TPU v7x, 128 devices: a whole 4x4x4 slice. The times are simulated.
128 devices in a mesh: tm: 8 (over x, core), sy: 4 (over z), sx: 4 (over y).
Axes of the slice: x: 4, y: 4, z: 4, core: 2. Of those that a mesh axis runs over, the one named last changes fastest.
Arguments:
- latent_init: float32 [64, 96, 320], P('sy', 'sx'), may hold values from -80 to 80
- step_noise: bfloat16 [32, 64, 96, 320], P('tm', 'sy', 'sx'), may hold values from -6 to 6
- coef_state: float32 [32], P('tm'), may hold values from -0.06 to -0.01
- coef_drift: float32 [32], P('tm'), may hold values from -0.1 to 0.1
- coef_noise: float32 [32], P('tm'), may hold values from 0.05 to 0.2
- step_index: int32 [32], P('tm'), may hold values from 0 to 999
- time_table: float32 [1000, 320], replicated, may hold values from -1.5 to 1.5
- norm_gain: float32 [320], replicated, may hold values from 0.25 to 1.75
- conv_weight: bfloat16 [3, 3, 320, 320], replicated, may hold values from -0.109375 to 0.109375
- reward_grad: float32 [64, 96, 320], P('sy', 'sx'), may hold values from -0.18 to 0.18
Outputs:
- trajectory: float32 [32, 64, 96, 320], P('tm', 'sy', 'sx')
- grad_weight: float32 [3, 3, 320, 320], P(None, None, None, 'tm')
All inputs are finite; a program needn't handle non-finite values.
Results may differ from a plain program's by a relative error of at most 0.0009.
The roundings to bfloat16 on the way count: a program that leaves them out, or rounds other values in their place, can miss the bound.
Values may be sent and summed in bfloat16 or wider, within the bound.
A program may use at most 128 MiB of HBM per device.

v0:
```python
import jax
import jax.numpy as jnp
from jax import lax
from jax.sharding import PartitionSpec as P

GROUPS = 32
ITERS = 2
EPSILON = 1e-05


def prefix(value, axis, join, neutral, backward):
    count, mine = (lax.axis_size(axis), lax.axis_index(axis))
    pieces = lax.all_gather(value, axis)
    if backward:
        pieces = pieces[::-1]
        mine = count - 1 - mine
    subtotal = jnp.full_like(value, 0) + jnp.asarray(neutral, value.dtype)

    def step(position, subtotal):
        longer = join(subtotal, pieces[position])
        return jnp.where(position < mine, longer, subtotal)

    return lax.fori_loop(0, count - 1, step, subtotal)


def with_halo(block, sides, width):
    for axis, dim in sides:
        count = lax.axis_size(axis)
        forward = [(i, i + 1) for i in range(count - 1)]
        backward = [(target, source) for source, target in forward]
        low = lax.ppermute(
            lax.slice_in_dim(block, block.shape[dim] - width, None, axis=dim), axis, forward
        )
        high = lax.ppermute(lax.slice_in_dim(block, 0, width, axis=dim), axis, backward)
        block = jnp.concatenate([low, block, high], axis=dim)
    return block


def add_terms(earlier, later):
    return earlier + later


def lower_total(block_total, reverse):
    return prefix(block_total, "tm", add_terms, jnp.zeros_like(block_total), reverse)


def group_count(tile_rows, tile_cols, channels):
    return tile_rows * lax.axis_size("sy") * tile_cols * lax.axis_size("sx") * (channels // GROUPS)


def group_stats(grouped, cell_count):
    totals = lax.psum(jnp.sum(grouped, axis=(1, 3)), ("sy", "sx"))
    center = totals / cell_count
    shifted = grouped - center[:, None, :, None]
    spread = lax.psum(jnp.sum(shifted * shifted, axis=(1, 3)), ("sy", "sx")) / cell_count
    return (shifted, spread)


def prepare(states, modulate):
    steps_here, tile_rows, tile_cols, channels = states.shape
    grouped = states.reshape(steps_here, tile_rows * tile_cols, GROUPS, channels // GROUPS)
    shifted, spread = group_stats(grouped, group_count(tile_rows, tile_cols, channels))
    inv_std = 1.0 / jnp.sqrt(spread + EPSILON)
    normal_field = (shifted * inv_std[:, None, :, None]).reshape(states.shape)
    pre_act = normal_field * modulate[:, None, None, :]
    activation = jax.nn.silu(pre_act).astype(jnp.bfloat16)
    act_pad = with_halo(activation, (("sy", 1), ("sx", 2)), 1)
    return (normal_field, inv_std, pre_act, act_pad)


def convolve(act_pad, conv_weight, tile_rows, tile_cols):
    result = jnp.zeros(
        act_pad.shape[:1] + (tile_rows, tile_cols, conv_weight.shape[3]), jnp.float32
    )
    for row_off in range(3):
        for col_off in range(3):
            window = act_pad[:, row_off : row_off + tile_rows, col_off : col_off + tile_cols, :]
            result = result + jnp.einsum(
                "bhwc,cd->bhwd",
                window,
                conv_weight[row_off, col_off],
                preferred_element_type=jnp.float32,
            )
    return result


def backprop(upstream, act_cache, modulate, conv_weight, need_state):
    normal_field, inv_std, pre_act, act_pad = act_cache
    steps_here, tile_rows, tile_cols, channels = upstream.shape
    up_half = upstream.astype(jnp.bfloat16)
    weight_rows = []
    for row_off in range(3):
        weight_cols = []
        for col_off in range(3):
            window = act_pad[:, row_off : row_off + tile_rows, col_off : col_off + tile_cols, :]
            weight_cols.append(
                jnp.einsum("bhwc,bhwd->cd", window, up_half, preferred_element_type=jnp.float32)
            )
        weight_rows.append(jnp.stack(weight_cols))
    grad_piece = jnp.stack(weight_rows)
    if not need_state:
        return (upstream, grad_piece)
    up_pad = with_halo(up_half, (("sy", 1), ("sx", 2)), 1)
    d_act = jnp.zeros(upstream.shape, jnp.float32)
    for row_off in range(3):
        for col_off in range(3):
            window = up_pad[
                :, 2 - row_off : 2 - row_off + tile_rows, 2 - col_off : 2 - col_off + tile_cols, :
            ]
            d_act = d_act + jnp.einsum(
                "bhwd,cd->bhwc",
                window,
                conv_weight[row_off, col_off],
                preferred_element_type=jnp.float32,
            )
    sig_value = jax.nn.sigmoid(pre_act)
    d_norm = d_act * sig_value * (1.0 + pre_act * (1.0 - sig_value)) * modulate[:, None, None, :]
    group_shape = (steps_here, tile_rows * tile_cols, GROUPS, channels // GROUPS)
    grouped_d = d_norm.reshape(group_shape)
    grouped_n = normal_field.reshape(group_shape)
    cell_count = group_count(tile_rows, tile_cols, channels)
    plain_sum, cross_sum = lax.psum(
        (jnp.sum(grouped_d, axis=(1, 3)), jnp.sum(grouped_d * grouped_n, axis=(1, 3))), ("sy", "sx")
    )
    plain_mean = plain_sum / cell_count
    cross_mean = cross_sum / cell_count
    d_group = (
        grouped_d - plain_mean[:, None, :, None] - grouped_n * cross_mean[:, None, :, None]
    ) * inv_std[:, None, :, None]
    return (upstream + d_group.reshape(upstream.shape), grad_piece)


def shards(
    latent_init,
    step_noise,
    coef_state,
    coef_drift,
    coef_noise,
    step_index,
    time_table,
    norm_gain,
    conv_weight,
    reward_grad,
):
    tile_rows, tile_cols = (step_noise.shape[1], step_noise.shape[2])
    table_ids = jnp.arange(time_table.shape[0], dtype=jnp.int32)
    one_hot = (step_index[:, None] == table_ids[None, :]).astype(jnp.float32)
    embedded = jnp.dot(one_hot, time_table, precision=lax.Precision.HIGHEST)
    modulate = norm_gain[None, :] * (1.0 + embedded)
    state_c = coef_state[:, None, None, None]
    drift_c = coef_drift[:, None, None, None]
    noise_c = coef_noise[:, None, None, None]
    states = jnp.broadcast_to(latent_init[None], step_noise.shape)
    saved_states = []
    caches = []
    trajectory = states
    for sweep_index in range(ITERS):
        saved_states.append(states)
        act_cache = prepare(states, modulate)
        caches.append(act_cache)
        drift_term = states + convolve(act_cache[3], conv_weight, tile_rows, tile_cols)
        increment = (
            state_c * states + drift_c * drift_term + noise_c * step_noise.astype(jnp.float32)
        )
        running = jnp.cumsum(increment, axis=0)
        offset = lower_total(running[-1], False)
        trajectory = latent_init[None] + (offset[None] + running)
        if sweep_index + 1 < ITERS:
            before = jnp.concatenate([jnp.zeros_like(running[:1]), running[:-1]], axis=0)
            states = latent_init[None] + (offset[None] + before)
    adjoint = jnp.broadcast_to(reward_grad[None], step_noise.shape)
    grad_total = jnp.zeros(conv_weight.shape, jnp.float32)
    for sweep_index in range(ITERS - 1, -1, -1):
        act_cache = prepare(saved_states[sweep_index], modulate)
        upstream = drift_c * adjoint
        d_state, grad_piece = backprop(upstream, act_cache, modulate, conv_weight, sweep_index > 0)
        grad_total = grad_total + grad_piece
        if sweep_index > 0:
            through = state_c * adjoint + d_state
            suffix = jnp.cumsum(through[::-1], axis=0)[::-1]
            higher = lower_total(suffix[0], True)
            after = jnp.concatenate([suffix[1:], jnp.zeros_like(suffix[:1])], axis=0)
            adjoint = higher[None] + after
    share = lax.psum_scatter(grad_total, "tm", scatter_dimension=3, tiled=True)
    grad_weight = lax.psum(share, ("sy", "sx"))
    return (trajectory, grad_weight)


def solution(mesh):
    placed = (
        P("sy", "sx", None),
        P("tm", "sy", "sx", None),
        P("tm"),
        P("tm"),
        P("tm"),
        P("tm"),
        P(),
        P(),
        P(),
        P("sy", "sx", None),
    )
    return jax.shard_map(
        shards,
        mesh=mesh,
        in_specs=placed,
        out_specs=(P("tm", "sy", "sx", None), P(None, None, None, "tm")),
        check_vma=False,
    )
```

profile of v0, /device:TPU:0, one launch (start us, length us, event | category | flops | bytes accessed | tf_op | source)
XLA Modules:
  0.0 634.3 jit_solution(18137577999258617183)
XLA Ops:
  8.7 42.0 %psum.46 = f32[4,32]{1,0:T(4,128)S(1)} all-reduce(f32[4,32]{1,0:T(4,128)S(1)} %reduce_sum.117), channel_id=1, replica_groups=mesh['tm'=8,'sy'=4,'sx'=4] {'sy','sx'}, use_global_device_ids=true, to_apply=%region_2.0 | all-reduce | flops 128 | bytes 1024 | tf_op jit(solution)/shard_map/psum | solution.py:52
  52.5 35.5 %psum.49 = f32[4,32]{1,0:T(4,128)S(1)} all-reduce(f32[4,32]{1,0:T(4,128)S(1)} %reduce_sum.120), channel_id=1, replica_groups=mesh['tm'=8,'sy'=4,'sx'=4] {'sy','sx'}, use_global_device_ids=true, to_apply=%region_5.6 | all-reduce | flops 128 | bytes 1024 | tf_op jit(solution)/shard_map/psum | solution.py:55
  98.3 3.9 collective-permute-start.2
  123.3 6.3 fusion.33
  142.3 4.7 collective-permute-start.11
  166.6 8.7 %while.42 = (s32[]{:T(128)}, f32[16,24,320]{2,1,0:T(8,128)S(1)}, s32[]{:T(128)}, f32[8,16,24,320]{3,2,1,0:T(8,128)}, s32[]{:T(128)}, /*index=5*/s32[]{:T(128)}) while((s32[]{:T(128)}, f32[16,24,320]{2,1,0:T(8,128)S(1)}, s32[]{:T(128)}, f32[8,16,24,320]{3,2,1,0:T(8,128)}, s32[]{:T(128)}, /*index=5*/s32[]{:T(128)}) %tuple.106), condition=%wide.region_8.9_spmd.clone, body=%wide.region_7.8_spmd.clone.sunk | while | flops 368644 | bytes 1474653 | solution.py:23
  177.3 39.5 %psum.50 = f32[4,32]{1,0:T(4,128)S(1)} all-reduce(f32[4,32]{1,0:T(4,128)S(1)} %reduce_sum.123), channel_id=1, replica_groups=mesh['tm'=8,'sy'=4,'sx'=4] {'sy','sx'}, use_global_device_ids=true, to_apply=%region_11.12 | all-reduce | flops 128 | bytes 1024 | tf_op jit(solution)/shard_map/psum | solution.py:52
  222.4 36.1 %psum.51 = f32[4,32]{1,0:T(4,128)} all-reduce(f32[4,32]{1,0:T(4,128)} %reduce_sum.126), channel_id=1, replica_groups=mesh['tm'=8,'sy'=4,'sx'=4] {'sy','sx'}, use_global_device_ids=true, to_apply=%region_14.15 | all-reduce | flops 128 | bytes 1024 | tf_op jit(solution)/shard_map/psum | solution.py:55
  261.5 11.5 %fusion.219 = (f32[4,320]{1,0:T(4,128)}, f32[4,320]{1,0:T(4,128)}, f32[4,16,24,320]{3,2,1,0:T(8,128)}) fusion(f32[4,320]{1,0:T(4,128)} %mul.201, f32[4,320]{1,0:T(4,128)S(1)} %sub.66, f32[3,16,24,320]{3,2,1,0:T(8,128)S(1)} %slice.280, f32[16,24,320]{2,1,0:T(8,128)S(1)} %get-tuple-element.239, f32[16,24,320]{2,1,0:T(8,128)S(1)} %copy-done.2, ...), kind=kOutput, calls=%fused_computation.276 | convolution fusion | flops 326858240 | bytes 24750080 | tf_op jit(solution)/shard_map/bhwd,cd->bhwc/dot_general | solution.py:110
  278.9 38.4 %all-reduce.3 = (f32[4,32]{1,0:T(4,128)}, f32[4,32]{1,0:T(4,128)}) all-reduce(f32[4,32]{1,0:T(4,128)} %reduce_sum.132, f32[4,32]{1,0:T(4,128)} %reduce_sum.129), channel_id=1, replica_groups=mesh['tm'=8,'sy'=4,'sx'=4] {'sy','sx'}, use_global_device_ids=true, to_apply=%region_23.24 | all-reduce | flops 256 | bytes 2048 | tf_op jit(solution)/shard_map/psum | solution.py:122
  323.7 5.2 fusion.18
  344.5 3.5 fusion.162
  356.8 3.8 fusion.146
  381.5 4.9 rev.8
  386.4 8.7 %while.44 = (s32[]{:T(128)}, f32[16,24,320]{2,1,0:T(8,128)S(1)}, s32[]{:T(128)}, f32[8,16,24,320]{3,2,1,0:T(8,128)}, s32[]{:T(128)}, /*index=5*/s32[]{:T(128)}) while((s32[]{:T(128)}, f32[16,24,320]{2,1,0:T(8,128)S(1)}, s32[]{:T(128)}, f32[8,16,24,320]{3,2,1,0:T(8,128)}, s32[]{:T(128)}, /*index=5*/s32[]{:T(128)}) %tuple.112), condition=%wide.region_26.27_spmd.clone, body=%wide.region_25.26_spmd.clone.sunk | while | flops 368644 | bytes 1474653 | solution.py:23
  410.1 8.4 %copy.14 = f32[3,3,320,320]{2,1,0,3:T(4,128)} copy(f32[3,3,320,320]{3,2,1,0:T(8,128)} %maximum_add_fusion) | data formatting | bytes 7372800 | tf_op jit(solution)/shard_map/add | solution.py:177
  419.1 3.9 fusion.113
  423.0 3.6 fusion.116
  430.0 3.5 fusion.122
  436.9 8.6 %fusion.19 = f32[4,16,24,320]{3,2,1,0:T(8,128)S(1)} fusion(f32[4,16,24,320]{3,2,1,0:T(8,128)} %fusion.110, f32[4,16,24,320]{3,2,1,0:T(8,128)} %fusion.145, f32[4,16,24,320]{3,2,1,0:T(8,128)} %fusion.113, f32[4,16,24,320]{3,2,1,0:T(8,128)} %fusion.116, f32[4,16,24,320]{3,2,1,0:T(8,128)} %fusion.162, f32[4,16,24,320]{3,2,1,0:T(8,128)} %fusion.119, ...), kind=kOutput, calls=%fused_computation.31 | output fusion | flops 9830400 | bytes 23101488 | tf_op jit(solution)/shard_map/jit(cumsum)/reduce_window_sum | solution.py:165
  449.1 50.9 %all-reduce.9.cloned.1.call-done = f32[3,3,320,320]{2,1,0,3:T(4,128)} async-done(((f32[3,3,320,320]{2,1,0,3:T(4,128)}), f32[3,3,320,320]{2,1,0,3:T(4,128)}) %all-reduce.9.cloned.1.call-update) | async-done | bytes 3686416
  502.2 33.7 %all-gather.6.cloned.1.call-done = f32[8,16,24,320]{3,2,1,0:T(8,128)} async-done(((f32[1,16,24,320]{3,2,1,0:T(8,128)}), f32[8,16,24,320]{3,2,1,0:T(8,128)}) %all-gather.6.cloned.1.call-update) | async-done | bytes 3932176 | tf_op jit(solution)/shard_map/all_gather | solution.py:13
  535.9 8.7 %while.43 = (s32[]{:T(128)}, f32[16,24,320]{2,1,0:T(8,128)S(1)}, s32[]{:T(128)}, f32[8,16,24,320]{3,2,1,0:T(8,128)}, s32[]{:T(128)}, /*index=5*/s32[]{:T(128)}) while((s32[]{:T(128)}, f32[16,24,320]{2,1,0:T(8,128)S(1)}, s32[]{:T(128)}, f32[8,16,24,320]{3,2,1,0:T(8,128)}, s32[]{:T(128)}, /*index=5*/s32[]{:T(128)}) %tuple.109), condition=%wide.region_17.18_spmd.clone, body=%wide.region_16.17_spmd.clone.sunk | while | flops 368644 | bytes 1474653 | solution.py:23
  548.0 77.7 %all-reduce.7.cloned.1.call-done = f32[3,3,320,40]{2,1,0,3:T(4,128)} async-done(((f32[3,3,320,40]{2,1,0,3:T(4,128)}), f32[3,3,320,40]{2,1,0,3:T(4,128)}) %all-reduce.7.cloned.1.call-update) | async-done | bytes 460816 | tf_op jit(solution)/shard_map/psum | solution.py:185
  (263 shorter events, 192.7 us)
Async XLA Ops:
  7.2 81.0 %copy-start = (f32[1000,320]{0,1:T(8,128)S(1)}, f32[1000,320]{0,1:T(8,128)}, u32[]{:S(2)}) copy-start(f32[1000,320]{0,1:T(8,128)} %param.22) | copy-start | bytes 3840004
  7.2 82.6 %copy-start.2 = (f32[16,24,320]{2,1,0:T(8,128)S(1)}, f32[16,24,320]{2,1,0:T(8,128)}, u32[]{:S(2)}) copy-start(f32[16,24,320]{2,1,0:T(8,128)} %param.16) | copy-start | bytes 1474564
  7.2 159.4 %all-gather.4.cloned.1.call-start = ((), (), s32[]{:S(2)}) async-start(), calls=%async_computation | async-start | bytes 5308416 | tf_op jit(solution)/shard_map/all_gather | solution.py:13
  51.0 44.8 %copy-start.39 = (f32[4,320]{1,0:T(4,128)}, f32[4,320]{1,0:T(4,128)S(1)}, u32[]{:S(2)}) copy-start(f32[4,320]{1,0:T(4,128)S(1)} %sub.62) | copy-start | bytes 15364
  90.5 18.4 %copy-start.5 = (bf16[4,16,24,320]{3,2,1,0:T(8,128)(2,1)}, bf16[4,16,24,320]{3,2,1,0:T(8,128)(2,1)S(1)}, u32[]{:S(2)}) copy-start(bf16[4,16,24,320]{3,2,1,0:T(8,128)(2,1)S(1)} %fusion.17) | copy-start | bytes 2949124
  90.5 5.2 collective-permute-start
  91.8 6.2 collective-permute-start.1
  95.8 13.1 %copy-start.32 = (bf16[4,1,24,320]{3,2,1,0:T(8,128)(2,1)}, bf16[4,1,24,320]{3,2,1,0:T(8,128)(2,1)S(1)}, u32[]{:S(2)}) copy-start(bf16[4,1,24,320]{3,2,1,0:T(8,128)(2,1)S(1)} %collective-permute-done) | copy-start | bytes 184324
  98.3 7.8 %collective-permute-start.2 = (bf16[4,18,1,320]{3,2,1,0:T(2,128)(2,1)S(1)}, bf16[4,18,1,320]{3,2,1,0:T(2,128)(2,1)S(1)}, u32[]{:S(2)}, u32[]{:S(2)}) collective-permute-start(bf16[4,18,1,320]{3,2,1,0:T(2,128)(2,1)S(1)} %get-tuple-element.333), channel_id=1, source_target_pairs={{0,1},{1,2},{2,3},{4,5},{5,6},{6,7},{8,9},{9,10},{10,11},{12,13},{... | collective-permute-start | bytes 138248 | tf_op jit(solution)/shard_map/ppermute | solution.py:31
  102.2 6.6 %collective-permute-start.3 = (bf16[4,18,1,320]{3,2,1,0:T(2,128)(2,1)S(1)}, bf16[4,18,1,320]{3,2,1,0:T(2,128)(2,1)S(1)}, u32[]{:S(2)}, u32[]{:S(2)}) collective-permute-start(bf16[4,18,1,320]{3,2,1,0:T(2,128)(2,1)S(1)} %get-tuple-element.334), channel_id=1, source_target_pairs={{1,0},{2,1},{3,2},{5,4},{6,5},{7,6},{9,8},{10,9},{11,10},{13,12},{... | collective-permute-start | bytes 138248 | tf_op jit(solution)/shard_map/ppermute | solution.py:34
  131.9 249.6 %all-gather.8.cloned.1.call-start = ((), (), s32[]{:S(2)}) async-start(), calls=%async_computation.2 | async-start | bytes 5308416 | tf_op jit(solution)/shard_map/all_gather | solution.py:13
  132.3 18.0 %copy-start.7 = (bf16[4,16,24,320]{3,2,1,0:T(8,128)(2,1)}, bf16[4,16,24,320]{3,2,1,0:T(8,128)(2,1)S(1)}, u32[]{:S(2)}) copy-start(bf16[4,16,24,320]{3,2,1,0:T(8,128)(2,1)S(1)} %multiply_convert_fusion) | copy-start | bytes 2949124
  132.3 6.9 %collective-permute-start.8 = (bf16[4,1,24,320]{3,2,1,0:T(8,128)(2,1)S(1)}, bf16[4,1,24,320]{3,2,1,0:T(8,128)(2,1)S(1)}, u32[]{:S(2)}, u32[]{:S(2)}) collective-permute-start(bf16[4,1,24,320]{3,2,1,0:T(8,128)(2,1)S(1)} %get-tuple-element.336), channel_id=1, source_target_pairs={{0,4},{4,8},{8,12},{1,5},{5,9},{9,13},{2,6},{6,10},{10,14},{3,7},{... | collective-permute-start | bytes 184328 | tf_op jit(solution)/shard_map/ppermute | solution.py:31
  134.6 6.2 collective-permute-start.9
  141.0 11.8 %collective-permute-start.10 = (bf16[4,18,1,320]{3,2,1,0:T(2,128)(2,1)S(1)}, bf16[4,18,1,320]{3,2,1,0:T(2,128)(2,1)S(1)}, u32[]{:S(2)}, u32[]{:S(2)}) collective-permute-start(bf16[4,18,1,320]{3,2,1,0:T(2,128)(2,1)S(1)} %get-tuple-element.326), channel_id=1, source_target_pairs={{1,0},{2,1},{3,2},{5,4},{6,5},{7,6},{9,8},{10,9},{11,10},{13,12},{... | collective-permute-start | bytes 138248 | tf_op jit(solution)/shard_map/ppermute | solution.py:34
  142.3 10.5 %collective-permute-start.11 = (bf16[4,18,1,320]{3,2,1,0:T(2,128)(2,1)S(1)}, bf16[4,18,1,320]{3,2,1,0:T(2,128)(2,1)S(1)}, u32[]{:S(2)}, u32[]{:S(2)}) collective-permute-start(bf16[4,18,1,320]{3,2,1,0:T(2,128)(2,1)S(1)} %get-tuple-element.325), channel_id=1, source_target_pairs={{0,1},{1,2},{2,3},{4,5},{5,6},{6,7},{8,9},{9,10},{10,11},{12,13},{... | collective-permute-start | bytes 138248 | tf_op jit(solution)/shard_map/ppermute | solution.py:31
  336.3 163.8 %all-reduce.9.cloned.1.call-start = ((), (), s32[]{:S(2)}) async-start(), calls=%async_computation.4 | async-start | bytes 11796480
  337.9 14.2 %collective-permute-start.4 = (bf16[4,1,24,320]{3,2,1,0:T(8,128)(2,1)}, bf16[4,1,24,320]{3,2,1,0:T(8,128)(2,1)}, u32[]{:S(2)}, u32[]{:S(2)}) collective-permute-start(bf16[4,1,24,320]{3,2,1,0:T(8,128)(2,1)} %get-tuple-element.337), channel_id=1, source_target_pairs={{0,4},{4,8},{8,12},{1,5},{5,9},{9,13},{2,6},{6,10},{10,14},{3,7},{... | collective-permute-start | bytes 184328 | tf_op jit(solution)/shard_map/ppermute | solution.py:31
  339.8 12.3 %collective-permute-start.5 = (bf16[4,1,24,320]{3,2,1,0:T(8,128)(2,1)}, bf16[4,1,24,320]{3,2,1,0:T(8,128)(2,1)}, u32[]{:S(2)}, u32[]{:S(2)}) collective-permute-start(bf16[4,1,24,320]{3,2,1,0:T(8,128)(2,1)} %get-tuple-element.338), channel_id=1, source_target_pairs={{4,0},{8,4},{12,8},{5,1},{9,5},{13,9},{6,2},{10,6},{14,10},{7,3},{... | collective-permute-start | bytes 184328 | tf_op jit(solution)/shard_map/ppermute | solution.py:34
  353.7 13.6 %collective-permute-start.6 = (bf16[4,18,1,320]{3,2,1,0:T(2,128)(2,1)S(1)}, bf16[4,18,1,320]{3,2,1,0:T(2,128)(2,1)S(1)}, u32[]{:S(2)}, u32[]{:S(2)}) collective-permute-start(bf16[4,18,1,320]{3,2,1,0:T(2,128)(2,1)S(1)} %get-tuple-element.329), channel_id=1, source_target_pairs={{0,1},{1,2},{2,3},{4,5},{5,6},{6,7},{8,9},{9,10},{10,11},{12,13},{... | collective-permute-start | bytes 138248 | tf_op jit(solution)/shard_map/ppermute | solution.py:31
  355.5 11.8 %collective-permute-start.7 = (bf16[4,18,1,320]{3,2,1,0:T(2,128)(2,1)S(1)}, bf16[4,18,1,320]{3,2,1,0:T(2,128)(2,1)S(1)}, u32[]{:S(2)}, u32[]{:S(2)}) collective-permute-start(bf16[4,18,1,320]{3,2,1,0:T(2,128)(2,1)S(1)} %get-tuple-element.330), channel_id=1, source_target_pairs={{1,0},{2,1},{3,2},{5,4},{6,5},{7,6},{9,8},{10,9},{11,10},{13,12},{... | collective-permute-start | bytes 138248 | tf_op jit(solution)/shard_map/ppermute | solution.py:34
  418.5 117.4 %all-gather.6.cloned.1.call-start = ((), (), s32[]{:S(2)}) async-start(), calls=%async_computation.1 | async-start | bytes 5308416 | tf_op jit(solution)/shard_map/all_gather | solution.py:13
  447.8 177.9 %all-reduce.7.cloned.1.call-start = ((), (), s32[]{:S(2)}) async-start(), calls=%async_computation.3 | async-start | bytes 1474560 | tf_op jit(solution)/shard_map/psum | solution.py:185
  544.6 83.0 %copy-start.1 = (f32[1000,320]{0,1:T(8,128)S(1)}, f32[1000,320]{0,1:T(8,128)}, u32[]{:S(2)}) copy-start(f32[1000,320]{0,1:T(8,128)} %param.22) | copy-start | bytes 3840004
  (43 other events, 196.2 us)
Sparse Core Ops, SparseCore 0:
  132.0 33.4 all-gather.3
  336.4 29.2 all-gather.7
  418.7 81.3 all-reduce.8
  501.7 34.1 all-gather.5
  539.4 86.2 all-reduce.6
where the time goes:
time: 641 us; the launch traced here: 634 us
  blocking collectives  191 us (30%)
  waiting for transfers between devices  169 us (26%)
  matrix products  101 us (16%)
  other arithmetic  78.4 us (12%)
  local copies, waits for them, and re-layouts  53.7 us (8%)
  starting transfers between devices  24.9 us (4%)
  between operations  15.4 us (2%)
    psum x2, blocking collectives, group_stats(): totals = lax.psum(jnp.sum(grouped, axis=(1, 3)), ('sy', 'sx'))  81.5 us
    psum x1, waiting for transfers between devices, shards(): grad_weight = lax.psum(share, ('sy', 'sx'))  77.7 us
    psum x2, blocking collectives, group_stats(): lax.psum(jnp.sum(shifted * shifted, axis=(1, 3)), ('sy', 'sx')) / cell_count  71.6 us
    unnamed x6, waiting for transfers between devices  51 us
    dot_general x18, matrix products, convolve(): jnp.einsum('bhwc,cd->bhwd', window, conv_weight[row_off, col_off], prefer...  49.6 us
    psum x1, blocking collectives, backprop(): lax.psum((jnp.sum(grouped_d, axis=(1, 3)), jnp.sum(grouped_d * grouped_n,...  38.4 us
    all_gather x3, waiting for transfers between devices, prefix(): pieces = lax.all_gather(value, axis)  33.7 us
    dot_general x9, matrix products, backprop(): jnp.einsum('bhwd,cd->bhwc', window, conv_weight[row_off, col_off], prefer...  31.9 us
  transfers between devices with their start and end apart: 17, of which 6 were waited for; matrix products, arithmetic and copies ran while one was open for 17% of the time, Pallas kernels for 0%

commit v1 on v0

--- a/solution.py
+++ b/solution.py
@@ -52,7 +52,12 @@
     totals = lax.psum(jnp.sum(grouped, axis=(1, 3)), ("sy", "sx"))
     center = totals / cell_count
     shifted = grouped - center[:, None, :, None]
-    spread = lax.psum(jnp.sum(shifted * shifted, axis=(1, 3)), ("sy", "sx")) / cell_count
+    spread = (
+        jax.lax.psum(
+            jax.lax.psum(jnp.sum(shifted * shifted, axis=(1, 3)), axis_name="sx"), axis_name="sy"
+        )
+        / cell_count
+    )
     return (shifted, spread)
 
 

time: 641 us -> 605 us (0.944)
  blocking collectives: 191 us -> 153 us
    psum x2 -> x4, blocking collectives: 71.6 us -> 32.9 us  [the longest x2 16.7 us: group_stats(): jax.lax.psum(jax.lax.psum(jnp.sum(shifted * shifted, axis=(1, 3)), axis_n...]
  transfers between devices with their start and end apart: 17 -> 17, of which waited for: 6 -> 6; matrix products, arithmetic and copies ran while one was open for 17% -> 18% of each run, Pallas kernels for 0% -> 0%
where the time goes in v1:
time: 605 us; the launch traced here: 598 us
  waiting for transfers between devices  170 us (28%)
  blocking collectives  153 us (25%)
  matrix products  101 us (17%)
  other arithmetic  78.5 us (13%)
  local copies, waits for them, and re-layouts  53.6 us (9%)
  starting transfers between devices  26.5 us (4%)
  between operations  15.5 us (3%)
    psum x2, blocking collectives, group_stats(): totals = lax.psum(jnp.sum(grouped, axis=(1, 3)), ('sy', 'sx'))  80.4 us
    psum x1, waiting for transfers between devices, shards(): grad_weight = lax.psum(share, ('sy', 'sx'))  77.7 us
    unnamed x6, waiting for transfers between devices  51.7 us
    dot_general x18, matrix products, convolve(): jnp.einsum('bhwc,cd->bhwd', window, conv_weight[row_off, col_off], prefer...  49.5 us
    psum x1, blocking collectives, backprop(): lax.psum((jnp.sum(grouped_d, axis=(1, 3)), jnp.sum(grouped_d * grouped_n,...  39.5 us
    all_gather x3, waiting for transfers between devices, prefix(): pieces = lax.all_gather(value, axis)  33.7 us
    dot_general x9, matrix products, backprop(): jnp.einsum('bhwd,cd->bhwc', window, conv_weight[row_off, col_off], prefer...  31.9 us
    select_n x21, other arithmetic, step(): return jnp.where(position < mine, longer, subtotal)  25.6 us
  transfers between devices with their start and end apart: 17, of which 6 were waited for; matrix products, arithmetic and copies ran while one was open for 18% of the time, Pallas kernels for 0%

profile of v1, /device:TPU:0, one launch (start us, length us, event | category | flops | bytes accessed | tf_op | source)
XLA Modules:
  0.0 597.8 jit_solution(4228413107425633821)
XLA Ops:
  8.7 42.0 %psum.60 = f32[4,32]{1,0:T(4,128)S(1)} all-reduce(f32[4,32]{1,0:T(4,128)S(1)} %reduce_sum.117), channel_id=1, replica_groups=mesh['tm'=8,'sy'=4,'sx'=4] {'sy','sx'}, use_global_device_ids=true, to_apply=%region_2.0 | all-reduce | flops 128 | bytes 1024 | tf_op jit(solution)/shard_map/psum | solution.py:52
  52.5 7.7 %psum.61 = f32[4,32]{1,0:T(4,128)S(1)} all-reduce(f32[4,32]{1,0:T(4,128)S(1)} %reduce_sum.120), channel_id=1, replica_groups=mesh['tm'=8,'sy'=4,'sx'=4] {'sx'}, use_global_device_ids=true, to_apply=%region_5.6 | all-reduce | flops 128 | bytes 1024 | tf_op jit(solution)/shard_map/psum | solution.py:57
  60.3 8.0 %psum.64 = f32[4,32]{1,0:T(4,128)S(1)} all-reduce(f32[4,32]{1,0:T(4,128)S(1)} %psum.61), channel_id=1, replica_groups=mesh['tm'=8,'sy'=4,'sx'=4] {'sy'}, use_global_device_ids=true, to_apply=%region_6.7 | all-reduce | flops 128 | bytes 1024 | tf_op jit(solution)/shard_map/psum | solution.py:56
  70.8 3.6 collective-permute-start
  80.9 3.9 collective-permute-start.2
  105.9 6.3 %fusion.33 = f32[4,16,24,320]{3,2,1,0:T(8,128)S(1)} fusion(bf16[4,16,24,320]{3,2,1,0:T(8,128)(2,1)} %param.17, f32[4,16,24,320]{3,2,1,0:T(8,128)S(1)} %fusion.128, f32[4,16,24,320]{3,2,1,0:T(8,128)S(1)} %fusion.147, f32[4,16,24,320]{3,2,1,0:T(8,128)} %fusion.131, f32[4,16,24,320]{3,2,1,0:T(8,128)} %fusion.134, f32[4,16,24,320]{3,2,1,0:T(8,128)} %fusion.164, ...), kind=kOutput, calls=%fused_computation.49 | output fusion | flops 8847360 | bytes 21135408 | tf_op jit(solution)/shard_map/jit(cumsum)/reduce_window_sum | solution.py:170
  125.0 4.7 collective-permute-start.11
  149.2 8.7 %while.42 = (s32[]{:T(128)}, f32[16,24,320]{2,1,0:T(8,128)S(1)}, s32[]{:T(128)}, f32[8,16,24,320]{3,2,1,0:T(8,128)}, s32[]{:T(128)}, /*index=5*/s32[]{:T(128)}) while((s32[]{:T(128)}, f32[16,24,320]{2,1,0:T(8,128)S(1)}, s32[]{:T(128)}, f32[8,16,24,320]{3,2,1,0:T(8,128)}, s32[]{:T(128)}, /*index=5*/s32[]{:T(128)}) %tuple.106), condition=%wide.region_9.10_spmd.clone, body=%wide.region_8.9_spmd.clone.sunk | while | flops 368644 | bytes 1474653 | solution.py:23
  159.8 38.4 %psum.65 = f32[4,32]{1,0:T(4,128)S(1)} all-reduce(f32[4,32]{1,0:T(4,128)S(1)} %reduce_sum.123), channel_id=1, replica_groups=mesh['tm'=8,'sy'=4,'sx'=4] {'sy','sx'}, use_global_device_ids=true, to_apply=%region_12.13 | all-reduce | flops 128 | bytes 1024 | tf_op jit(solution)/shard_map/psum | solution.py:52
  203.9 8.4 %psum.66 = f32[4,32]{1,0:T(4,128)} all-reduce(f32[4,32]{1,0:T(4,128)} %reduce_sum.126), channel_id=1, replica_groups=mesh['tm'=8,'sy'=4,'sx'=4] {'sx'}, use_global_device_ids=true, to_apply=%region_15.16 | all-reduce | flops 128 | bytes 1024 | tf_op jit(solution)/shard_map/psum | solution.py:57
  212.3 8.7 %psum.69 = f32[4,32]{1,0:T(4,128)} all-reduce(f32[4,32]{1,0:T(4,128)} %psum.66), channel_id=1, replica_groups=mesh['tm'=8,'sy'=4,'sx'=4] {'sy'}, use_global_device_ids=true, to_apply=%region_16.17 | all-reduce | flops 128 | bytes 1024 | tf_op jit(solution)/shard_map/psum | solution.py:56
  224.0 11.5 %fusion.219 = (f32[4,320]{1,0:T(4,128)}, f32[4,320]{1,0:T(4,128)}, f32[4,16,24,320]{3,2,1,0:T(8,128)}) fusion(f32[4,320]{1,0:T(4,128)} %mul.201, f32[4,320]{1,0:T(4,128)S(1)} %sub.66, f32[3,16,24,320]{3,2,1,0:T(8,128)S(1)} %slice.280, f32[16,24,320]{2,1,0:T(8,128)S(1)} %get-tuple-element.239, f32[16,24,320]{2,1,0:T(8,128)S(1)} %copy-done.2, ...), kind=kOutput, calls=%fused_computation.276 | convolution fusion | flops 326858240 | bytes 24750080 | tf_op jit(solution)/shard_map/bhwd,cd->bhwc/dot_general | solution.py:115
  241.3 39.5 %all-reduce.3 = (f32[4,32]{1,0:T(4,128)}, f32[4,32]{1,0:T(4,128)}) all-reduce(f32[4,32]{1,0:T(4,128)} %reduce_sum.132, f32[4,32]{1,0:T(4,128)} %reduce_sum.129), channel_id=1, replica_groups=mesh['tm'=8,'sy'=4,'sx'=4] {'sy','sx'}, use_global_device_ids=true, to_apply=%region_25.26 | all-reduce | flops 256 | bytes 2048 | tf_op jit(solution)/shard_map/psum | solution.py:127
  287.3 5.2 fusion.18
  319.9 3.8 fusion.146
  344.8 4.9 rev.8
  349.7 8.7 %while.44 = (s32[]{:T(128)}, f32[16,24,320]{2,1,0:T(8,128)S(1)}, s32[]{:T(128)}, f32[8,16,24,320]{3,2,1,0:T(8,128)}, s32[]{:T(128)}, /*index=5*/s32[]{:T(128)}) while((s32[]{:T(128)}, f32[16,24,320]{2,1,0:T(8,128)S(1)}, s32[]{:T(128)}, f32[8,16,24,320]{3,2,1,0:T(8,128)}, s32[]{:T(128)}, /*index=5*/s32[]{:T(128)}) %tuple.112), condition=%wide.region_28.29_spmd.clone, body=%wide.region_27.28_spmd.clone.sunk | while | flops 368644 | bytes 1474653 | solution.py:23
  373.3 8.4 %copy.14 = f32[3,3,320,320]{2,1,0,3:T(4,128)} copy(f32[3,3,320,320]{3,2,1,0:T(8,128)} %maximum_add_fusion) | data formatting | bytes 7372800 | tf_op jit(solution)/shard_map/add | solution.py:182
  382.0 3.9 fusion.113
  399.7 8.6 %fusion.19 = f32[4,16,24,320]{3,2,1,0:T(8,128)S(1)} fusion(f32[4,16,24,320]{3,2,1,0:T(8,128)} %fusion.110, f32[4,16,24,320]{3,2,1,0:T(8,128)} %fusion.145, f32[4,16,24,320]{3,2,1,0:T(8,128)} %fusion.113, f32[4,16,24,320]{3,2,1,0:T(8,128)} %fusion.116, f32[4,16,24,320]{3,2,1,0:T(8,128)} %fusion.162, f32[4,16,24,320]{3,2,1,0:T(8,128)} %fusion.119, ...), kind=kOutput, calls=%fused_computation.31 | output fusion | flops 9830400 | bytes 23101488 | tf_op jit(solution)/shard_map/jit(cumsum)/reduce_window_sum | solution.py:170
  411.9 51.7 %all-reduce.9.cloned.1.call-done = f32[3,3,320,320]{2,1,0,3:T(4,128)} async-done(((f32[3,3,320,320]{2,1,0,3:T(4,128)}), f32[3,3,320,320]{2,1,0,3:T(4,128)}) %all-reduce.9.cloned.1.call-update) | async-done | bytes 3686416
  465.7 33.7 %all-gather.6.cloned.1.call-done = f32[8,16,24,320]{3,2,1,0:T(8,128)} async-done(((f32[1,16,24,320]{3,2,1,0:T(8,128)}), f32[8,16,24,320]{3,2,1,0:T(8,128)}) %all-gather.6.cloned.1.call-update) | async-done | bytes 3932176 | tf_op jit(solution)/shard_map/all_gather | solution.py:13
  499.4 8.7 %while.43 = (s32[]{:T(128)}, f32[16,24,320]{2,1,0:T(8,128)S(1)}, s32[]{:T(128)}, f32[8,16,24,320]{3,2,1,0:T(8,128)}, s32[]{:T(128)}, /*index=5*/s32[]{:T(128)}) while((s32[]{:T(128)}, f32[16,24,320]{2,1,0:T(8,128)S(1)}, s32[]{:T(128)}, f32[8,16,24,320]{3,2,1,0:T(8,128)}, s32[]{:T(128)}, /*index=5*/s32[]{:T(128)}) %tuple.109), condition=%wide.region_19.20_spmd.clone, body=%wide.region_18.19_spmd.clone.sunk | while | flops 368644 | bytes 1474653 | solution.py:23
  511.4 77.7 %all-reduce.7.cloned.1.call-done = f32[3,3,320,40]{2,1,0,3:T(4,128)} async-done(((f32[3,3,320,40]{2,1,0,3:T(4,128)}), f32[3,3,320,40]{2,1,0,3:T(4,128)}) %all-reduce.7.cloned.1.call-update) | async-done | bytes 460816 | tf_op jit(solution)/shard_map/psum | solution.py:190
  (265 shorter events, 201.2 us)
Async XLA Ops:
  7.2 61.3 %copy-start = (f32[1000,320]{0,1:T(8,128)S(1)}, f32[1000,320]{0,1:T(8,128)}, u32[]{:S(2)}) copy-start(f32[1000,320]{0,1:T(8,128)} %param.22) | copy-start | bytes 3840004
  7.2 62.9 %copy-start.2 = (f32[16,24,320]{2,1,0:T(8,128)S(1)}, f32[16,24,320]{2,1,0:T(8,128)}, u32[]{:S(2)}) copy-start(f32[16,24,320]{2,1,0:T(8,128)} %param.16) | copy-start | bytes 1474564
  7.2 142.0 %all-gather.4.cloned.1.call-start = ((), (), s32[]{:S(2)}) async-start(), calls=%async_computation | async-start | bytes 5308416 | tf_op jit(solution)/shard_map/all_gather | solution.py:13
  51.0 27.4 %copy-start.39 = (f32[4,320]{1,0:T(4,128)}, f32[4,320]{1,0:T(4,128)S(1)}, u32[]{:S(2)}) copy-start(f32[4,320]{1,0:T(4,128)S(1)} %sub.62) | copy-start | bytes 15364
  70.8 20.7 %copy-start.5 = (bf16[4,16,24,320]{3,2,1,0:T(8,128)(2,1)}, bf16[4,16,24,320]{3,2,1,0:T(8,128)(2,1)S(1)}, u32[]{:S(2)}) copy-start(bf16[4,16,24,320]{3,2,1,0:T(8,128)(2,1)S(1)} %fusion.17) | copy-start | bytes 2949124
  70.8 7.6 %collective-permute-start = (bf16[4,1,24,320]{3,2,1,0:T(8,128)(2,1)S(1)}, bf16[4,1,24,320]{3,2,1,0:T(8,128)(2,1)S(1)}, u32[]{:S(2)}, u32[]{:S(2)}) collective-permute-start(bf16[4,1,24,320]{3,2,1,0:T(8,128)(2,1)S(1)} %get-tuple-element.339), channel_id=1, source_target_pairs={{0,4},{4,8},{8,12},{1,5},{5,9},{9,13},{2,6},{6,10},{10,14},{3,7},{... | collective-permute-start | bytes 184328 | tf_op jit(solution)/shard_map/ppermute | solution.py:31
  74.5 6.2 %collective-permute-start.1 = (bf16[4,1,24,320]{3,2,1,0:T(8,128)(2,1)S(1)}, bf16[4,1,24,320]{3,2,1,0:T(8,128)(2,1)S(1)}, u32[]{:S(2)}, u32[]{:S(2)}) collective-permute-start(bf16[4,1,24,320]{3,2,1,0:T(8,128)(2,1)S(1)} %get-tuple-element.340), channel_id=1, source_target_pairs={{4,0},{8,4},{12,8},{5,1},{9,5},{13,9},{6,2},{10,6},{14,10},{7,3},{... | collective-permute-start | bytes 184328 | tf_op jit(solution)/shard_map/ppermute | solution.py:34
  78.4 13.1 %copy-start.32 = (bf16[4,1,24,320]{3,2,1,0:T(8,128)(2,1)}, bf16[4,1,24,320]{3,2,1,0:T(8,128)(2,1)S(1)}, u32[]{:S(2)}) copy-start(bf16[4,1,24,320]{3,2,1,0:T(8,128)(2,1)S(1)} %collective-permute-done) | copy-start | bytes 184324
  80.9 7.7 %collective-permute-start.2 = (bf16[4,18,1,320]{3,2,1,0:T(2,128)(2,1)S(1)}, bf16[4,18,1,320]{3,2,1,0:T(2,128)(2,1)S(1)}, u32[]{:S(2)}, u32[]{:S(2)}) collective-permute-start(bf16[4,18,1,320]{3,2,1,0:T(2,128)(2,1)S(1)} %get-tuple-element.333), channel_id=1, source_target_pairs={{0,1},{1,2},{2,3},{4,5},{5,6},{6,7},{8,9},{9,10},{10,11},{12,13},{... | collective-permute-start | bytes 138248 | tf_op jit(solution)/shard_map/ppermute | solution.py:31
  84.8 6.6 %collective-permute-start.3 = (bf16[4,18,1,320]{3,2,1,0:T(2,128)(2,1)S(1)}, bf16[4,18,1,320]{3,2,1,0:T(2,128)(2,1)S(1)}, u32[]{:S(2)}, u32[]{:S(2)}) collective-permute-start(bf16[4,18,1,320]{3,2,1,0:T(2,128)(2,1)S(1)} %get-tuple-element.334), channel_id=1, source_target_pairs={{1,0},{2,1},{3,2},{5,4},{6,5},{7,6},{9,8},{10,9},{11,10},{13,12},{... | collective-permute-start | bytes 138248 | tf_op jit(solution)/shard_map/ppermute | solution.py:34
  114.5 230.3 %all-gather.8.cloned.1.call-start = ((), (), s32[]{:S(2)}) async-start(), calls=%async_computation.2 | async-start | bytes 5308416 | tf_op jit(solution)/shard_map/all_gather | solution.py:13
  114.9 18.0 %copy-start.7 = (bf16[4,16,24,320]{3,2,1,0:T(8,128)(2,1)}, bf16[4,16,24,320]{3,2,1,0:T(8,128)(2,1)S(1)}, u32[]{:S(2)}) copy-start(bf16[4,16,24,320]{3,2,1,0:T(8,128)(2,1)S(1)} %multiply_convert_fusion) | copy-start | bytes 2949124
  114.9 6.9 %collective-permute-start.8 = (bf16[4,1,24,320]{3,2,1,0:T(8,128)(2,1)S(1)}, bf16[4,1,24,320]{3,2,1,0:T(8,128)(2,1)S(1)}, u32[]{:S(2)}, u32[]{:S(2)}) collective-permute-start(bf16[4,1,24,320]{3,2,1,0:T(8,128)(2,1)S(1)} %get-tuple-element.336), channel_id=1, source_target_pairs={{0,4},{4,8},{8,12},{1,5},{5,9},{9,13},{2,6},{6,10},{10,14},{3,7},{... | collective-permute-start | bytes 184328 | tf_op jit(solution)/shard_map/ppermute | solution.py:31
  117.2 6.2 %collective-permute-start.9 = (bf16[4,1,24,320]{3,2,1,0:T(8,128)(2,1)S(1)}, bf16[4,1,24,320]{3,2,1,0:T(8,128)(2,1)S(1)}, u32[]{:S(2)}, u32[]{:S(2)}) collective-permute-start(bf16[4,1,24,320]{3,2,1,0:T(8,128)(2,1)S(1)} %get-tuple-element.335), channel_id=1, source_target_pairs={{4,0},{8,4},{12,8},{5,1},{9,5},{13,9},{6,2},{10,6},{14,10},{7,3},{... | collective-permute-start | bytes 184328 | tf_op jit(solution)/shard_map/ppermute | solution.py:34
  123.7 11.8 %collective-permute-start.10 = (bf16[4,18,1,320]{3,2,1,0:T(2,128)(2,1)S(1)}, bf16[4,18,1,320]{3,2,1,0:T(2,128)(2,1)S(1)}, u32[]{:S(2)}, u32[]{:S(2)}) collective-permute-start(bf16[4,18,1,320]{3,2,1,0:T(2,128)(2,1)S(1)} %get-tuple-element.326), channel_id=1, source_target_pairs={{1,0},{2,1},{3,2},{5,4},{6,5},{7,6},{9,8},{10,9},{11,10},{13,12},{... | collective-permute-start | bytes 138248 | tf_op jit(solution)/shard_map/ppermute | solution.py:34
  125.0 10.5 %collective-permute-start.11 = (bf16[4,18,1,320]{3,2,1,0:T(2,128)(2,1)S(1)}, bf16[4,18,1,320]{3,2,1,0:T(2,128)(2,1)S(1)}, u32[]{:S(2)}, u32[]{:S(2)}) collective-permute-start(bf16[4,18,1,320]{3,2,1,0:T(2,128)(2,1)S(1)} %get-tuple-element.325), channel_id=1, source_target_pairs={{0,1},{1,2},{2,3},{4,5},{5,6},{6,7},{8,9},{9,10},{10,11},{12,13},{... | collective-permute-start | bytes 138248 | tf_op jit(solution)/shard_map/ppermute | solution.py:31
  299.9 163.7 %all-reduce.9.cloned.1.call-start = ((), (), s32[]{:S(2)}) async-start(), calls=%async_computation.4 | async-start | bytes 11796480
  301.5 14.3 %collective-permute-start.4 = (bf16[4,1,24,320]{3,2,1,0:T(8,128)(2,1)}, bf16[4,1,24,320]{3,2,1,0:T(8,128)(2,1)}, u32[]{:S(2)}, u32[]{:S(2)}) collective-permute-start(bf16[4,1,24,320]{3,2,1,0:T(8,128)(2,1)} %get-tuple-element.337), channel_id=1, source_target_pairs={{0,4},{4,8},{8,12},{1,5},{5,9},{9,13},{2,6},{6,10},{10,14},{3,7},{... | collective-permute-start | bytes 184328 | tf_op jit(solution)/shard_map/ppermute | solution.py:31
  303.5 12.4 %collective-permute-start.5 = (bf16[4,1,24,320]{3,2,1,0:T(8,128)(2,1)}, bf16[4,1,24,320]{3,2,1,0:T(8,128)(2,1)}, u32[]{:S(2)}, u32[]{:S(2)}) collective-permute-start(bf16[4,1,24,320]{3,2,1,0:T(8,128)(2,1)} %get-tuple-element.338), channel_id=1, source_target_pairs={{4,0},{8,4},{12,8},{5,1},{9,5},{13,9},{6,2},{10,6},{14,10},{7,3},{... | collective-permute-start | bytes 184328 | tf_op jit(solution)/shard_map/ppermute | solution.py:34
  317.3 13.1 %collective-permute-start.6 = (bf16[4,18,1,320]{3,2,1,0:T(2,128)(2,1)S(1)}, bf16[4,18,1,320]{3,2,1,0:T(2,128)(2,1)S(1)}, u32[]{:S(2)}, u32[]{:S(2)}) collective-permute-start(bf16[4,18,1,320]{3,2,1,0:T(2,128)(2,1)S(1)} %get-tuple-element.329), channel_id=1, source_target_pairs={{0,1},{1,2},{2,3},{4,5},{5,6},{6,7},{8,9},{9,10},{10,11},{12,13},{... | collective-permute-start | bytes 138248 | tf_op jit(solution)/shard_map/ppermute | solution.py:31
  318.6 11.8 %collective-permute-start.7 = (bf16[4,18,1,320]{3,2,1,0:T(2,128)(2,1)S(1)}, bf16[4,18,1,320]{3,2,1,0:T(2,128)(2,1)S(1)}, u32[]{:S(2)}, u32[]{:S(2)}) collective-permute-start(bf16[4,18,1,320]{3,2,1,0:T(2,128)(2,1)S(1)} %get-tuple-element.330), channel_id=1, source_target_pairs={{1,0},{2,1},{3,2},{5,4},{6,5},{7,6},{9,8},{10,9},{11,10},{13,12},{... | collective-permute-start | bytes 138248 | tf_op jit(solution)/shard_map/ppermute | solution.py:34
  381.7 117.7 %all-gather.6.cloned.1.call-start = ((), (), s32[]{:S(2)}) async-start(), calls=%async_computation.1 | async-start | bytes 5308416 | tf_op jit(solution)/shard_map/all_gather | solution.py:13
  410.6 178.6 %all-reduce.7.cloned.1.call-start = ((), (), s32[]{:S(2)}) async-start(), calls=%async_computation.3 | async-start | bytes 1474560 | tf_op jit(solution)/shard_map/psum | solution.py:190
  508.1 83.0 %copy-start.1 = (f32[1000,320]{0,1:T(8,128)S(1)}, f32[1000,320]{0,1:T(8,128)}, u32[]{:S(2)}) copy-start(f32[1000,320]{0,1:T(8,128)} %param.22) | copy-start | bytes 3840004
  (43 other events, 199.7 us)
Sparse Core Ops, SparseCore 0:
  114.6 32.3 all-gather.3
  300.0 29.2 all-gather.7
  381.8 81.6 all-reduce.8
  465.2 34.1 all-gather.5
  502.9 86.2 all-reduce.6
